TPU v7x, 128 devices: a whole 4x4x4 slice. The times are simulated.
128 devices in a mesh: cand: 8 (over x_hi, z), prompt: 16 (over x_lo, y, core).
Axes of the slice: x: 4 (x_hi: 2, x_lo: 2; x = x_hi * 2 + x_lo), y: 4, z: 4, core: 2. Of those that a mesh axis runs over, the one named last changes fastest.
Arguments:
- hidden_states: bfloat16 [16, 8, 128, 4096], P('prompt', 'cand'), may hold values from -8 to 8
- proj_weight: bfloat16 [4096, 1024], P(('cand', 'prompt')), may hold values from -0.0625 to 0.0625
- bilinear: bfloat16 [1024, 1024], P(('cand', 'prompt')), may hold values from -0.005859375 to 0.005859375
- lengths: int32 [16, 8], P('prompt'), may hold values from 32 to 128, as said below
- labels: int32 [16, 28], P('prompt'), may hold values 0 or 1
Outputs:
- pair_logits: float32 [16, 8, 8], P('prompt')
- grad_proj: float32 [4096, 1024], P(('cand', 'prompt'))
- grad_bilinear: float32 [1024, 1024], P(('cand', 'prompt'))
Inputs may be any that keep to these rules, and one draw needn't show every extreme that they name: `lengths`: every prompt has a candidate with all 128 rows valid.
All inputs are finite; a program needn't handle non-finite values. No bound on the sum of `labels` on one device may be relied on, other than what follows from the above.
Results may differ from a plain program's by a relative error of at most 0.0045.
Values may be sent and summed in bfloat16 or wider, within the bound.
No kernel may reach another device: no remote copies, remote signals or barrier semaphores. Data moves between devices by JAX's collectives and lax.ppermute only.
A program may use at most 128 MiB of HBM per device.

v0:
```python
import jax
import jax.numpy as jnp
import numpy as np
from jax import lax
from jax.sharding import PartitionSpec as P

HEADS = 16
HEAD_DIM = 64
EPSILON = 1e-06
HIGH = lax.Precision.HIGHEST


def shifted_2(value, axis, steps):
    count = lax.axis_size(axis)
    pairs = [(source, (source + steps) % count) for source in range(count)]
    return lax.ppermute(value, axis, pairs)


def attend_block(queries, keys, key_valid, factor):
    prompts, rows, width = queries.shape
    query_heads = queries.reshape(prompts, rows, HEADS, HEAD_DIM)
    key_heads = keys.reshape(prompts, rows, HEADS, HEAD_DIM)
    scores = (
        jnp.einsum("pthd,pshd->phts", query_heads, key_heads, preferred_element_type=jnp.float32)
        * factor
    )
    scores = jnp.where(key_valid[:, None, None, :], scores, -jnp.inf)
    shifted = jnp.exp(scores - jnp.max(scores, axis=3, keepdims=True))
    weights = shifted / jnp.sum(shifted, axis=3, keepdims=True)
    mixed = jnp.einsum(
        "phts,pshd->pthd",
        weights.astype(jnp.bfloat16),
        key_heads,
        preferred_element_type=jnp.float32,
    )
    return (weights, mixed)


def body(hidden_states, proj_weight, bilinear, lengths, labels):
    cands = lax.axis_size("cand")
    here = lax.axis_index("cand")
    prompts = hidden_states.shape[0]
    rows = hidden_states.shape[2]
    width = hidden_states.shape[3]
    inner = proj_weight.shape[1]
    factor = HEAD_DIM ** (-0.5)
    flat = hidden_states.reshape(prompts * rows, width)
    columns = flat
    projected = jnp.dot(
        columns,
        lax.all_gather(proj_weight, ("cand", "prompt"), axis=0, tiled=True),
        preferred_element_type=jnp.float32,
    )
    own_rows = projected.astype(jnp.bfloat16).reshape(prompts, rows, inner)
    own_heads = own_rows.reshape(prompts, rows, HEADS, HEAD_DIM)
    cand_ids = jnp.arange(cands, dtype=jnp.int32)
    positions = jnp.arange(rows, dtype=jnp.int32)

    def length_of(source):
        return jnp.sum(jnp.where(cand_ids[None, :] == source, lengths, 0), axis=1)

    own_length = length_of(here)
    own_valid = positions[None, :] < own_length[:, None]
    own_length_f = own_length.astype(jnp.float32)
    received = {}
    moving = own_rows
    for offset in range(1, cands):
        moving = shifted_2(moving, "cand", 1)
        received[offset] = moving
    sources = {}
    means = {}
    radii = {}
    pooled = jnp.zeros((prompts, cands, inner), jnp.float32)
    for offset in range(1, cands):
        source = (here - offset) % cands
        other_valid = positions[None, :] < length_of(source)[:, None]
        weights, mixed = attend_block(own_rows, received[offset], other_valid, factor)
        total = jnp.sum(jnp.where(own_valid[:, :, None, None], mixed, 0.0), axis=1)
        mean_row = total.reshape(prompts, inner) / own_length_f[:, None]
        radius = jnp.sqrt(jnp.mean(mean_row * mean_row, axis=1, keepdims=True) + EPSILON)
        normed = mean_row / radius
        pooled = pooled + jnp.where((cand_ids == source)[None, :, None], normed[:, None, :], 0.0)
        sources[offset] = source
        means[offset] = mean_row
        radii[offset] = radius
    everything = lax.all_gather(pooled[:, None], "cand", axis=1, tiled=True)
    full_bil = lax.all_gather(bilinear, ("cand", "prompt"), axis=0, tiled=True).astype(jnp.float32)
    toward = jnp.einsum("ab,pjib->pija", full_bil, everything, precision=HIGH)
    pair_logits = jnp.sum(everything * toward, axis=3)
    upper_i, upper_j = np.triu_indices(cands, 1)
    wins = labels.astype(jnp.float32)
    target = (
        jnp.zeros((prompts, cands, cands), jnp.float32)
        .at[:, upper_i, upper_j]
        .set(wins)
        .at[:, upper_j, upper_i]
        .set(1.0 - wins)
    )
    offdiag = 1.0 - jnp.eye(cands, dtype=jnp.float32)
    sign = 2.0 * target - 1.0
    dlogit = -sign * jax.nn.sigmoid(-sign * pair_logits) * offdiag[None]
    backward_dir = jnp.einsum("ba,pjib->pija", full_bil, everything, precision=HIGH)
    dpooled = dlogit[..., None] * toward + jnp.swapaxes(dlogit, 1, 2)[..., None] * backward_dir
    own_mask = cand_ids == here
    dnormed_own = jnp.sum(jnp.where(own_mask[None, :, None, None], dpooled, 0.0), axis=1)
    reverse_pool = jnp.sum(jnp.where(own_mask[None, None, :, None], everything, 0.0), axis=2)
    own_dlogit = jnp.sum(jnp.where(own_mask[None, :, None], dlogit, 0.0), axis=1)
    bil_term = jnp.einsum("pj,pja,pjb->ab", own_dlogit, pooled, reverse_pool, precision=HIGH)
    grad_bilinear = lax.psum_scatter(bil_term, ("cand", "prompt"), scatter_dimension=0, tiled=True)
    row_weight = jnp.where(own_valid, 1.0, 0.0) / own_length_f[:, None]
    query_grads = jnp.zeros((prompts, rows, inner), jnp.float32)
    owners = jnp.zeros((cands, prompts, rows, inner), jnp.float32)
    for offset in range(1, cands):
        backward_source = sources[offset]
        others = received[offset]
        backward_other_valid = positions[None, :] < length_of(backward_source)[:, None]
        backward_weights, unused = attend_block(own_rows, others, backward_other_valid, factor)
        dnorm = jnp.sum(
            jnp.where((cand_ids == backward_source)[None, :, None], dnormed_own, 0.0), axis=1
        )
        norm_row = means[offset] / radii[offset]
        dmean = (dnorm - norm_row * jnp.mean(dnorm * norm_row, axis=1, keepdims=True)) / radii[
            offset
        ]
        dmean_heads = dmean.reshape(prompts, HEADS, HEAD_DIM)
        other_heads = others.reshape(prompts, rows, HEADS, HEAD_DIM)
        along = jnp.einsum(
            "pshd,phd->phs", other_heads.astype(jnp.float32), dmean_heads, precision=HIGH
        )
        expected = jnp.einsum("phts,phs->pht", backward_weights, along, precision=HIGH)
        dscore = (
            row_weight[:, None, :, None]
            * backward_weights
            * (along[:, :, None, :] - expected[:, :, :, None])
            * factor
        )
        dscore = dscore.astype(jnp.bfloat16)
        dquery = jnp.einsum(
            "phts,pshd->pthd", dscore, other_heads, preferred_element_type=jnp.float32
        )
        column = jnp.einsum("phts,pt->phs", backward_weights, row_weight, precision=HIGH)
        dkey = jnp.einsum(
            "phts,pthd->pshd", dscore, own_heads, preferred_element_type=jnp.float32
        ) + jnp.einsum("phs,phd->pshd", column, dmean_heads, precision=HIGH)
        dquery, dkey, source = (
            dquery.reshape(prompts, rows, inner),
            dkey.reshape(prompts, rows, inner),
            backward_source,
        )
        query_grads = query_grads + dquery
        owners = owners + jnp.where((cand_ids == source)[:, None, None, None], dkey[None], 0.0)
    home = lax.psum_scatter(owners, "cand", scatter_dimension=0, tiled=True)[0]
    total_grad = (query_grads + home).astype(jnp.bfloat16).reshape(prompts * rows, inner)
    columns = flat
    grad_proj = lax.psum_scatter(
        lax.dot_general(
            columns, total_grad, (((0,), (0,)), ((), ())), preferred_element_type=jnp.float32
        ),
        ("cand", "prompt"),
        scatter_dimension=0,
        tiled=True,
    )
    return (pair_logits, grad_proj, grad_bilinear)


def solution(mesh):
    in_specs = (
        P("prompt", "cand", None, None),
        P(("cand", "prompt"), None),
        P(("cand", "prompt"), None),
        P("prompt", None),
        P("prompt", None),
    )
    out_specs = (P("prompt", None, None), P(("cand", "prompt"), None), P(("cand", "prompt"), None))
    return jax.shard_map(body, mesh=mesh, in_specs=in_specs, out_specs=out_specs, check_vma=False)
```

profile of v0, /device:TPU:0, one launch (start us, length us, event | category | flops | bytes accessed | tf_op | source)
XLA Modules:
  0.0 1861.5 jit_solution(6400430401243026478)
XLA Ops:
  18.1 197.4 %all-gather.3.cloned.1.call-done = bf16[4096,1024]{1,0:T(8,128)(2,1)} async-done(((bf16[32,1024]{1,0:T(8,128)(2,1)}), bf16[4096,1024]{1,0:T(8,128)(2,1)}) %all-gather.3.cloned.1.call-update) | async-done | bytes 8388624 | tf_op jit(solution)/shard_map/all_gather | solution.py:51
  215.5 4.6 convolution_convert_fusion
  226.5 5.1 collective-permute-done
  235.9 8.7 collective-permute-done.1
  249.1 9.9 collective-permute-done.2
  267.2 3.0 fusion.144
  270.1 7.4 collective-permute-done.3
  283.1 10.1 collective-permute-done.4
  300.9 3.0 fusion.140
  303.8 7.4 collective-permute-done.5
  316.8 6.8 collective-permute-done.6
  331.3 36.6 %all_gather.10 = f32[1,8,8,1024]{3,2,0,1:T(8,128)} all-gather(f32[1,1,8,1024]{3,2,0,1:T(8,128)S(1)} %select_add_fusion.1), channel_id=1, replica_groups=mesh['cand'=8,'prompt'=16] {'cand'}, dimensions={1}, use_global_device_ids=true | all-gather | bytes 294912 | tf_op jit(solution)/shard_map/all_gather | solution.py:86
  368.0 3.0 fusion.136
  370.9 48.1 %all-gather.5.cloned.1.call-done = bf16[1024,1024]{1,0:T(8,128)(2,1)} async-done(((bf16[8,1024]{1,0:T(8,128)(2,1)}), bf16[1024,1024]{1,0:T(8,128)(2,1)}) %all-gather.5.cloned.1.call-update) | async-done | bytes 2097168 | tf_op jit(solution)/shard_map/all_gather | solution.py:87
  419.0 4.4 select_reduce_fusion
  424.1 2.9 fusion.40
  442.8 2.5 fusion.108
  460.4 5.0 select_add_fusion
  465.4 5.8 fusion.77
  477.9 70.6 %reduce-scatter.6.cloned.1.call-done = f32[1,1,128,1024]{2,3,1,0:T(8,128)} async-done(((f32[8,1,128,1024]{2,3,1,0:T(8,128)}), f32[1,1,128,1024]{2,3,1,0:T(8,128)}) %reduce-scatter.6.cloned.1.call-update) | async-done | bytes 524304 | tf_op jit(solution)/shard_map/reduce_scatter | solution.py:152
  548.5 9.1 convolution_bitcast_fusion
  557.6 17.5 copy.271
  575.1 617.9 %reduce-scatter.8.cloned.1.call-done = f32[8,1024]{1,0:T(8,128)} async-done(((f32[1024,1024]{1,0:T(8,128)}), f32[8,1024]{1,0:T(8,128)}) %reduce-scatter.8.cloned.1.call-update) | async-done | bytes 32784 | tf_op jit(solution)/shard_map/reduce_scatter | solution.py:109
  1193.0 661.6 %reduce-scatter.10.cloned.1.call-done = f32[32,1024]{1,0:T(8,128)} async-done(((f32[4096,1024]{1,0:T(8,128)}), f32[32,1024]{1,0:T(8,128)}) %reduce-scatter.10.cloned.1.call-update) | async-done | bytes 131088
  (413 shorter events, 87.5 us)
Async XLA Ops:
  7.2 208.3 %copy-start = (bf16[1,1,128,4096]{3,2,1,0:T(8,128)(2,1)S(1)}, bf16[1,1,128,4096]{3,2,1,0:T(8,128)(2,1)}, u32[]{:S(2)}) copy-start(bf16[1,1,128,4096]{3,2,1,0:T(8,128)(2,1)} %param.11) | copy-start | bytes 3145732
  7.2 208.3 %all-gather.3.cloned.1.call-start = ((), (), s32[]{:S(2)}) async-start(), calls=%async_computation.3 | async-start | bytes 8454144 | tf_op jit(solution)/shard_map/all_gather | solution.py:51
  7.9 411.1 %all-gather.5.cloned.1.call-start = ((), (), s32[]{:S(2)}) async-start(), calls=%async_computation.4 | async-start | bytes 2113536 | tf_op jit(solution)/shard_map/all_gather | solution.py:87
  8.7 539.8 %reduce-scatter.6.cloned.1.call-start = ((), (), s32[]{:S(2)}) async-start(), calls=%async_computation.5 | async-start | bytes 4718592 | tf_op jit(solution)/shard_map/reduce_scatter | solution.py:152
  10.2 321.0 %copy-start.90 = (pred[8]{0:T(512)(128)(4,1)}, pred[8]{0:T(512)(128)(4,1)S(1)}, u32[]{:S(2)}) copy-start(pred[8]{0:T(512)(128)(4,1)S(1)} %iota_compare_fusion.16) | copy-start | bytes 28
  10.2 321.0 %copy-start.57 = (pred[8]{0:T(512)(128)(4,1)}, pred[8]{0:T(512)(128)(4,1)S(1)}, u32[]{:S(2)}) copy-start(pred[8]{0:T(512)(128)(4,1)S(1)} %get-tuple-element.62) | copy-start | bytes 28
  10.2 321.0 %copy-start.59 = (pred[8]{0:T(512)(128)(4,1)}, pred[8]{0:T(512)(128)(4,1)S(1)}, u32[]{:S(2)}) copy-start(pred[8]{0:T(512)(128)(4,1)S(1)} %get-tuple-element.63) | copy-start | bytes 28
  13.0 269.6 %copy-start.133 = (pred[128]{0:T(512)(128)(4,1)}, pred[128]{0:T(512)(128)(4,1)S(1)}, u32[]{:S(2)}) copy-start(pred[128]{0:T(512)(128)(4,1)S(1)} %iota_compare_fusion.15) | copy-start | bytes 388
  14.4 266.5 %copy-start.108 = (f32[128]{0:T(128)}, f32[128]{0:T(128)S(1)}, u32[]{:S(2)}) copy-start(f32[128]{0:T(128)S(1)} %select_divide_fusion) | copy-start | bytes 1540
  18.1 204.2 %copy-start.34 = (s32[28]{0:T(128)S(1)}, s32[28]{0:T(128)}, u32[]{:S(2)}) copy-start(s32[28]{0:T(128)} %constant.182) | copy-start | bytes 340
  18.1 206.2 %copy-start.33 = (s32[28]{0:T(128)S(1)}, s32[28]{0:T(128)}, u32[]{:S(2)}) copy-start(s32[28]{0:T(128)} %constant.194) | copy-start | bytes 340
  220.2 11.5 collective-permute-start
  226.3 104.9 %copy-start.61 = (pred[8]{0:T(512)(128)(4,1)}, pred[8]{0:T(512)(128)(4,1)S(1)}, u32[]{:S(2)}) copy-start(pred[8]{0:T(512)(128)(4,1)S(1)} %get-tuple-element.60) | copy-start | bytes 28
  226.3 104.9 %copy-start.63 = (pred[8]{0:T(512)(128)(4,1)}, pred[8]{0:T(512)(128)(4,1)S(1)}, u32[]{:S(2)}) copy-start(pred[8]{0:T(512)(128)(4,1)S(1)} %get-tuple-element.61) | copy-start | bytes 28
  226.4 104.9 %copy-start.65 = (pred[8]{0:T(512)(128)(4,1)}, pred[8]{0:T(512)(128)(4,1)S(1)}, u32[]{:S(2)}) copy-start(pred[8]{0:T(512)(128)(4,1)S(1)} %get-tuple-element.58) | copy-start | bytes 28
  226.4 104.9 %copy-start.67 = (pred[8]{0:T(512)(128)(4,1)}, pred[8]{0:T(512)(128)(4,1)S(1)}, u32[]{:S(2)}) copy-start(pred[8]{0:T(512)(128)(4,1)S(1)} %get-tuple-element.59) | copy-start | bytes 28
  234.0 10.6 collective-permute-start.1
  248.7 10.4 collective-permute-start.2
  266.4 11.1 collective-permute-start.3
  282.6 10.6 collective-permute-start.4
  300.6 10.6 collective-permute-start.5
  313.0 10.6 collective-permute-start.6
  465.4 727.7 %reduce-scatter.8.cloned.1.call-start = ((), (), s32[]{:S(2)}) async-start(), calls=%async_computation.6 | async-start | bytes 4227072 | tf_op jit(solution)/shard_map/reduce_scatter | solution.py:109
  471.4 1383.3 %reduce-scatter.10.cloned.1.call-start = ((), (), s32[]{:S(2)}) async-start(), calls=%async_computation.7 | async-start | bytes 16908288
  (124 other events, 536.9 us)
Sparse Core Ops, SparseCore 0:
  9.7 205.7 all-gather.2
  217.2 201.7 all-gather.4
  465.5 82.9 reduce-scatter.5
  551.4 641.5 reduce-scatter.7
  1195.8 658.7 reduce-scatter.9
where the time goes:
time: 1870 us; the launch traced here: 1860 us
  waiting for transfers between devices  1650 us (88%)
  matrix products  79.6 us (4%)
  local copies, waits for them, and re-layouts  39.8 us (2%)
  blocking collectives  36.6 us (2%)
  between operations  25.7 us (1%)
  other arithmetic  25.1 us (1%)
    unnamed x6, waiting for transfers between devices  663 us
    reduce_scatter x1, waiting for transfers between devices, body(): lax.psum_scatter(bil_term, ('cand', 'prompt'), scatter_dimension=0, tiled...  618 us
    all_gather x1, waiting for transfers between devices, body(): lax.all_gather(proj_weight, ('cand', 'prompt'), axis=0, tiled=True)  197 us
    reduce_scatter x1, waiting for transfers between devices, body(): home = lax.psum_scatter(owners, 'cand', scatter_dimension=0, tiled=True)[0]  70.6 us
    ppermute x7, waiting for transfers between devices, shifted_2(): return lax.ppermute(value, axis, pairs)  55.3 us
    all_gather x1, waiting for transfers between devices, body(): lax.all_gather(bilinear, ('cand', 'prompt'), axis=0, tiled=True)  48.1 us
  transfers between devices with their start and end apart: 12, of which 12 were waited for; matrix products, arithmetic and copies ran while one was open for 5% of the time, Pallas kernels for 0%

commit v1 on v0

--- a/solution.py
+++ b/solution.py
@@ -48,7 +48,15 @@
     columns = flat
     projected = jnp.dot(
         columns,
-        lax.all_gather(proj_weight, ("cand", "prompt"), axis=0, tiled=True),
+        jnp.concatenate(
+            lax.all_to_all(
+                jnp.stack([proj_weight] * lax.axis_size(("cand", "prompt"))),
+                ("cand", "prompt"),
+                0,
+                0,
+            ),
+            axis=0,
+        ),
         preferred_element_type=jnp.float32,
     )
     own_rows = projected.astype(jnp.bfloat16).reshape(prompts, rows, inner)

time: 1870 us -> 1760 us (0.941)
  waiting for transfers between devices: 1650 us -> 1520 us
    all_gather x1 -> x0, waiting for transfers between devices: 197 us -> none  [body(): lax.all_gather(proj_weight, ('cand', 'prompt'), axis=0, tiled=True)]
    all_to_all x0 -> x1, waiting for transfers between devices: none -> 101 us  [body(): lax.all_to_all(jnp.stack([proj_weight] * lax.axis_size(('cand', 'prompt')...]
    all_gather x1, waiting for transfers between devices: 48.1 us -> 11.1 us  [body(): lax.all_gather(bilinear, ('cand', 'prompt'), axis=0, tiled=True)]
    unnamed x6 -> x5, waiting for transfers between devices: 663 us -> 664 us
  transfers between devices with their start and end apart: 12 -> 12, of which waited for: 12 -> 12; matrix products, arithmetic and copies ran while one was open for 5% -> 6% of each run, Pallas kernels for 0% -> 0%
where the time goes in v1:
time: 1760 us; the launch traced here: 1750 us
  waiting for transfers between devices  1520 us (86%)
  matrix products  79.7 us (5%)
  local copies, waits for them, and re-layouts  45.1 us (3%)
  blocking collectives  36.7 us (2%)
  between operations  26 us (1%)
  other arithmetic  23.1 us (1%)
    unnamed x5, waiting for transfers between devices  664 us
    reduce_scatter x1, waiting for transfers between devices, body(): lax.psum_scatter(bil_term, ('cand', 'prompt'), scatter_dimension=0, tiled...  620 us
    all_to_all x1, waiting for transfers between devices, body(): lax.all_to_all(jnp.stack([proj_weight] * lax.axis_size(('cand', 'prompt')...  101 us
    reduce_scatter x1, waiting for transfers between devices, body(): home = lax.psum_scatter(owners, 'cand', scatter_dimension=0, tiled=True)[0]  70.5 us
    ppermute x7, waiting for transfers between devices, shifted_2(): return lax.ppermute(value, axis, pairs)  56.1 us
    all_gather x1, blocking collectives, body(): everything = lax.all_gather(pooled[:, None], 'cand', axis=1, tiled=True)  36.7 us
  transfers between devices with their start and end apart: 12, of which 12 were waited for; matrix products, arithmetic and copies ran while one was open for 6% of the time, Pallas kernels for 0%

profile of v1, /device:TPU:0, one launch (start us, length us, event | category | flops | bytes accessed | tf_op | source)
XLA Modules:
  0.0 1746.4 jit_solution(14594481187534811226)
XLA Ops:
  7.2 5.2 stack.2
  12.4 11.7 all-to-all-start
  32.0 101.3 %all-to-all-done = bf16[128,32,1024]{2,1,0:T(8,128)(2,1)} async-done(((bf16[128,32,1024]{2,1,0:T(8,128)(2,1)}), bf16[128,32,1024]{2,1,0:T(8,128)(2,1)}, u32[]{:S(2)}, u32[]{:S(2)}) %all-to-all-start) | async-done | bytes 8388640 | tf_op jit(solution)/shard_map/all_to_all | solution.py:52
  133.3 4.7 convolution_convert_fusion
  143.4 6.1 collective-permute-done
  153.9 8.7 collective-permute-done.1
  167.2 9.8 collective-permute-done.2
  185.2 3.0 fusion.144
  188.2 7.4 collective-permute-done.3
  201.1 9.9 collective-permute-done.4
  218.8 2.9 fusion.140
  221.8 7.4 collective-permute-done.5
  234.7 6.7 collective-permute-done.6
  249.4 36.7 %all_gather.6 = f32[1,8,8,1024]{3,2,0,1:T(8,128)} all-gather(f32[1,1,8,1024]{3,2,0,1:T(8,128)S(1)} %select_add_fusion.1), channel_id=1, replica_groups=mesh['cand'=8,'prompt'=16] {'cand'}, dimensions={1}, use_global_device_ids=true | all-gather | bytes 294912 | tf_op jit(solution)/shard_map/all_gather | solution.py:94
  286.1 2.9 fusion.136
  289.1 11.1 all-gather.2.cloned.1.call-done
  300.2 4.4 select_reduce_fusion
  341.7 5.0 select_add_fusion
  346.8 5.9 fusion.77
  359.3 70.5 %reduce-scatter.6.cloned.1.call-done = f32[1,1,128,1024]{2,3,1,0:T(8,128)} async-done(((f32[8,1,128,1024]{2,3,1,0:T(8,128)}), f32[1,1,128,1024]{2,3,1,0:T(8,128)}) %reduce-scatter.6.cloned.1.call-update) | async-done | bytes 524304 | tf_op jit(solution)/shard_map/reduce_scatter | solution.py:160
  429.8 9.1 convolution_bitcast_fusion
  438.9 17.5 %copy.271 = f32[4096,1024]{1,0:T(8,128)} copy(f32[4096,1024]{0,1:T(8,128)} %convolution_bitcast_fusion) | data formatting | bytes 33554432
  456.4 619.8 %reduce-scatter.8.cloned.1.call-done = f32[8,1024]{1,0:T(8,128)} async-done(((f32[1024,1024]{1,0:T(8,128)}), f32[8,1024]{1,0:T(8,128)}) %reduce-scatter.8.cloned.1.call-update) | async-done | bytes 32784 | tf_op jit(solution)/shard_map/reduce_scatter | solution.py:117
  1076.2 663.4 %reduce-scatter.10.cloned.1.call-done = f32[32,1024]{1,0:T(8,128)} async-done(((f32[4096,1024]{1,0:T(8,128)}), f32[32,1024]{1,0:T(8,128)}) %reduce-scatter.10.cloned.1.call-update) | async-done | bytes 131088
  (417 shorter events, 89.3 us)
Async XLA Ops:
  7.2 126.1 %copy-start = (bf16[1,1,128,4096]{3,2,1,0:T(8,128)(2,1)S(1)}, bf16[1,1,128,4096]{3,2,1,0:T(8,128)(2,1)}, u32[]{:S(2)}) copy-start(bf16[1,1,128,4096]{3,2,1,0:T(8,128)(2,1)} %param.11) | copy-start | bytes 3145732
  12.4 120.9 %all-to-all-start = ((bf16[128,32,1024]{2,1,0:T(8,128)(2,1)}), bf16[128,32,1024]{2,1,0:T(8,128)(2,1)}, u32[]{:S(2)}, u32[]{:S(2)}) async-start(bf16[128,32,1024]{2,1,0:T(8,128)(2,1)} %stack.2), calls=%async_computation | async-start | bytes 16777216 | tf_op jit(solution)/shard_map/all_to_all | solution.py:52
  24.1 276.1 %all-gather.2.cloned.1.call-start = ((), (), s32[]{:S(2)}) async-start(), calls=%async_computation.4 | async-start | bytes 2113536 | tf_op jit(solution)/shard_map/all_gather | solution.py:95
  24.8 404.9 %reduce-scatter.6.cloned.1.call-start = ((), (), s32[]{:S(2)}) async-start(), calls=%async_computation.5 | async-start | bytes 4718592 | tf_op jit(solution)/shard_map/reduce_scatter | solution.py:160
  26.4 222.9 %copy-start.90 = (pred[8]{0:T(512)(128)(4,1)}, pred[8]{0:T(512)(128)(4,1)S(1)}, u32[]{:S(2)}) copy-start(pred[8]{0:T(512)(128)(4,1)S(1)} %iota_compare_fusion.16) | copy-start | bytes 28
  26.9 173.7 %copy-start.135 = (pred[128]{0:T(512)(128)(4,1)}, pred[128]{0:T(512)(128)(4,1)S(1)}, u32[]{:S(2)}) copy-start(pred[128]{0:T(512)(128)(4,1)S(1)} %iota_compare_fusion.15) | copy-start | bytes 388
  28.2 170.8 %copy-start.110 = (f32[128]{0:T(128)}, f32[128]{0:T(128)S(1)}, u32[]{:S(2)}) copy-start(f32[128]{0:T(128)S(1)} %select_divide_fusion) | copy-start | bytes 1540
  32.0 217.3 %copy-start.57 = (pred[8]{0:T(512)(128)(4,1)}, pred[8]{0:T(512)(128)(4,1)S(1)}, u32[]{:S(2)}) copy-start(pred[8]{0:T(512)(128)(4,1)S(1)} %get-tuple-element.62) | copy-start | bytes 28
  32.0 217.3 %copy-start.59 = (pred[8]{0:T(512)(128)(4,1)}, pred[8]{0:T(512)(128)(4,1)S(1)}, u32[]{:S(2)}) copy-start(pred[8]{0:T(512)(128)(4,1)S(1)} %get-tuple-element.63) | copy-start | bytes 28
  138.0 11.5 collective-permute-start
  143.2 106.1 %copy-start.61 = (pred[8]{0:T(512)(128)(4,1)}, pred[8]{0:T(512)(128)(4,1)S(1)}, u32[]{:S(2)}) copy-start(pred[8]{0:T(512)(128)(4,1)S(1)} %get-tuple-element.60) | copy-start | bytes 28
  143.2 106.1 %copy-start.63 = (pred[8]{0:T(512)(128)(4,1)}, pred[8]{0:T(512)(128)(4,1)S(1)}, u32[]{:S(2)}) copy-start(pred[8]{0:T(512)(128)(4,1)S(1)} %get-tuple-element.61) | copy-start | bytes 28
  143.2 106.1 %copy-start.65 = (pred[8]{0:T(512)(128)(4,1)}, pred[8]{0:T(512)(128)(4,1)S(1)}, u32[]{:S(2)}) copy-start(pred[8]{0:T(512)(128)(4,1)S(1)} %get-tuple-element.58) | copy-start | bytes 28
  143.2 106.1 %copy-start.67 = (pred[8]{0:T(512)(128)(4,1)}, pred[8]{0:T(512)(128)(4,1)S(1)}, u32[]{:S(2)}) copy-start(pred[8]{0:T(512)(128)(4,1)S(1)} %get-tuple-element.59) | copy-start | bytes 28
  152.0 10.6 collective-permute-start.1
  166.7 10.3 collective-permute-start.2
  184.5 11.1 collective-permute-start.3
  200.7 10.4 collective-permute-start.4
  218.6 10.6 collective-permute-start.5
  230.9 10.5 collective-permute-start.6
  244.6 44.4 %copy-start.49 = (f32[16,128]{1,0:T(8,128)}, f32[16,128]{1,0:T(8,128)S(1)}, u32[]{:S(2)}) copy-start(f32[16,128]{1,0:T(8,128)S(1)} %get-tuple-element.37) | copy-start | bytes 24580
  245.6 43.4 %copy-start.87 = (f32[16,128]{1,0:T(8,128)}, f32[16,128]{1,0:T(8,128)S(1)}, u32[]{:S(2)}) copy-start(f32[16,128]{1,0:T(8,128)S(1)} %fusion.58) | copy-start | bytes 24580
  346.7 729.5 %reduce-scatter.8.cloned.1.call-start = ((), (), s32[]{:S(2)}) async-start(), calls=%async_computation.6 | async-start | bytes 4227072 | tf_op jit(solution)/shard_map/reduce_scatter | solution.py:117
  352.8 1386.9 %reduce-scatter.10.cloned.1.call-start = ((), (), s32[]{:S(2)}) async-start(), calls=%async_computation.7 | async-start | bytes 16908288
  (126 other events, 496.2 us)
Sparse Core Ops, SparseCore 0:
  26.6 273.4 all-gather.1
  346.8 82.8 reduce-scatter.5
  432.8 643.3 reduce-scatter.7
  1079.0 660.5 reduce-scatter.9
